TPU v7x, 256 devices: a whole 4x4x8 slice. The times are simulated.
256 devices in a mesh: term: 16 (over z, core), doc: 16 (over y, x).
Axes of the slice: x: 4, y: 4, z: 8, core: 2. Of those that a mesh axis runs over, the one named last changes fastest.
Arguments:
- tile_values: bfloat16 [768, 2048, 128], P('term', 'doc'), may hold values from 0.001 to 1, as said below
- tile_rows: int32 [16, 768], P('term', 'doc'), may hold values from 0 to 15, as said below
- tile_cols: int32 [16, 768], P('term', 'doc'), may hold values from 0 to 15, as said below
- tile_count: int32 [16, 16], P('term', 'doc'), may hold values from 16 to 48, as said below
- start_block: bfloat16 [32768, 256], P('doc'), may hold values from -6 to 6
Outputs:
- row_scale: float32 [32768], P('term')
- col_scale: float32 [32768], P('doc')
- left_basis: bfloat16 [32768, 256], P('term')
- right_basis: bfloat16 [32768, 256], P('doc')
Inputs may be any that keep to these rules, and one draw needn't show every extreme that they name: `tile_values`: entries are positive. `tile_rows`: within one block pair the occupied (row, column) pairs are distinct, and every tile row and tile column of every block pair holds an occupied tile. `tile_cols`: paired with tile_rows slot by slot. `tile_count`: some block pair has all 48 slots occupied.
All inputs are finite; a program needn't handle non-finite values.
Results may differ from a plain program's by a relative error of at most 0.006.
The roundings to bfloat16 on the way count: a program that leaves them out, or rounds other values in their place, can miss the bound.
Values may be sent and summed in bfloat16 or wider, within the bound.
No kernel may reach another device: no remote copies, remote signals or barrier semaphores. Data moves between devices by JAX's collectives and lax.ppermute only.
A program may use at most 64 MiB of HBM per device.

v0:
```python
import math
import jax
import jax.numpy as jnp
from jax import lax
from jax.sharding import Mesh
from jax.sharding import PartitionSpec as P

TILE = 128
K = 256
PASSES = 2
RB = 16
CB = 16
TERM = ("term_0", "term_1")
DOC = ("doc_0", "doc_1")
PRECISE = lax.Precision.HIGHEST


def by_axis(shard, axes):
    for axis in axes:
        shard = lax.psum(shard, axis)
    return shard


def sent_to_all(shard, axis):
    copies = jnp.broadcast_to(shard, (lax.axis_size(axis), *shard.shape))
    return lax.all_to_all(copies, axis, split_axis=0, concat_axis=0, tiled=True)


def of_everyone(shard, axis):
    return sent_to_all(shard, axis).sum(axis=0)


def split_up(shard, dim, count):
    before, after = (shard.shape[:dim], shard.shape[dim + 1 :])
    return jnp.moveaxis(shard.reshape(*before, count, -1, *after), dim, 0)


def summed_on_arrival(shard, axis, dim):
    pieces = split_up(shard, dim, lax.axis_size(axis))
    arrived = lax.all_to_all(pieces, axis, split_axis=0, concat_axis=0, tiled=True)
    return arrived.sum(axis=0)


def filled_up(lines, count):
    spare = -lines.shape[0] % count
    if not spare:
        return lines
    return jnp.concatenate([lines, jnp.zeros((spare, *lines.shape[1:]), lines.dtype)])


def joined_along(pieces, dim):
    shape = list(pieces.shape[1:])
    shape[dim] *= pieces.shape[0]
    return jnp.moveaxis(pieces, 0, dim).reshape(shape)


def gather_directly(shard, axis, dim):
    return joined_along(sent_to_all(shard, axis), dim)


def sum_by_parts(shard, axes):
    own = summed_on_arrival(filled_up(shard, lax.axis_size(axes)), axes, 0)
    whole = gather_directly(own, axes, 0)
    return whole[: len(shard)].reshape(shard.shape)


def in_one(arrays, axis):
    ends = [0]
    for a in arrays:
        ends.append(ends[-1] + a.size)
    so_far = sum_by_parts(jnp.concatenate([a.ravel() for a in arrays]), axis)
    return tuple((so_far[b:e].reshape(a.shape) for a, b, e in zip(arrays, ends, ends[1:])))


def summed_rows(shard, axes, dim):
    far, near = axes
    pieces = split_up(shard, dim, lax.axis_size(far))
    nearer = summed_on_arrival(pieces, near, dim + 1)
    arrived = lax.all_to_all(nearer, far, split_axis=0, concat_axis=0, tiled=True)
    return arrived.sum(axis=0)


def gathered_by_axis(shard, axes, dim):
    far, near = axes
    pieces = sent_to_all(sent_to_all(shard, far), near)
    return joined_along(pieces.swapaxes(0, 1).reshape(-1, *shard.shape), dim)


def sum_by_parts_2(shard, axes):
    own = summed_rows(filled_up(shard, lax.axis_size(axes[0]) * lax.axis_size(axes[1])), axes, 0)
    whole = gathered_by_axis(own, axes, 0)
    return whole[: len(shard)].reshape(shard.shape)


def packed_total(arrays, axis):
    ends = [0]
    for a in arrays:
        ends.append(ends[-1] + a.size)
    so_far = sum_by_parts_2(jnp.concatenate([a.ravel() for a in arrays]), axis)
    return tuple((so_far[b:e].reshape(a.shape) for a, b, e in zip(arrays, ends, ends[1:])))


def total_of(shard, axes):
    lines = shard.reshape(-1, shard.shape[-1])
    own = summed_rows(filled_up(lines, lax.axis_size(axes[0]) * lax.axis_size(axes[1])), axes, 0)
    whole = gathered_by_axis(own, axes, 0)
    return whole[: len(lines)].reshape(shard.shape)


def factor_inverse(gram):
    lower = jnp.linalg.cholesky(gram)
    identity = jnp.eye(gram.shape[0], dtype=gram.dtype)
    return jax.scipy.linalg.solve_triangular(lower, identity, lower=True).T


def over_tiles(tile_values, row_ids, col_ids, occupied, advance, initial):
    slot_total = tile_values.shape[0]
    group_size = math.gcd(slot_total, 32)

    def visit(turn_index, running):
        offset = turn_index * group_size
        tile_block = lax.dynamic_slice_in_dim(tile_values, offset, group_size, 0)
        row_block = lax.dynamic_slice_in_dim(row_ids, offset, group_size, 0)
        col_block = lax.dynamic_slice_in_dim(col_ids, offset, group_size, 0)
        live_mask = (offset + jnp.arange(group_size, dtype=jnp.int32) < occupied).astype(
            jnp.float32
        )
        return advance(running, tile_block, row_block, col_block, live_mask)

    turn_total = slot_total // group_size
    return lax.fori_loop(0, turn_total, visit, initial)


def row_vector(source):

    def advance(running, tile_block, row_block, col_block, live_mask):
        picked = jnp.take(source, col_block, axis=0)
        product = jnp.einsum(
            "gab,gb->ga", tile_block.astype(jnp.float32), picked, precision=PRECISE
        )
        return running.at[row_block].add(product * live_mask[:, None])

    return advance


def col_vector(source):

    def advance(running, tile_block, row_block, col_block, live_mask):
        picked = jnp.take(source, row_block, axis=0)
        product = jnp.einsum(
            "gab,ga->gb", tile_block.astype(jnp.float32), picked, precision=PRECISE
        )
        return running.at[col_block].add(product * live_mask[:, None])

    return advance


def row_matrix(source):

    def advance(running, tile_block, row_block, col_block, live_mask):
        picked = jnp.take(source, col_block, axis=0)
        product = jnp.einsum("gab,gbk->gak", tile_block, picked, preferred_element_type=jnp.float32)
        return running.at[row_block].add(product * live_mask[:, None, None])

    return advance


def col_matrix(source):

    def advance(running, tile_block, row_block, col_block, live_mask):
        picked = jnp.take(source, row_block, axis=0)
        product = jnp.einsum("gab,gak->gbk", tile_block, picked, preferred_element_type=jnp.float32)
        return running.at[col_block].add(product * live_mask[:, None, None])

    return advance


def per_device(tile_values, tile_rows, tile_cols, tile_count, start_block):
    row_list = tile_rows[0]
    col_list = tile_cols[0]
    occupied = tile_count[0, 0]
    terms_total = RB * TILE * lax.axis_size(TERM)
    docs_total = CB * TILE * lax.axis_size(DOC)

    def tile_pass(advance, initial):
        return over_tiles(tile_values, row_list, col_list, occupied, advance, initial)

    col_scale = jnp.ones((CB, TILE), jnp.float32)
    row_scale = jnp.ones((RB, TILE), jnp.float32)
    mean_part = jnp.sum(start_block.astype(jnp.float32), axis=0)
    start_mean = mean_part
    for sweep_index in range(PASSES):
        row_part = tile_pass(row_vector(col_scale), jnp.zeros((RB, TILE), jnp.float32))
        if sweep_index == 0:
            row_total, start_mean = (by_axis(row_part, DOC), by_axis(mean_part, DOC))
        else:
            row_total = by_axis(row_part, DOC)
        row_scale = 1.0 / row_total
        col_part = tile_pass(col_vector(row_scale), jnp.zeros((CB, TILE), jnp.float32))
        col_scale = 1.0 / of_everyone(col_part, TERM)
    weight_part = tile_pass(row_vector(col_scale), jnp.zeros((RB, TILE), jnp.float32)).reshape(-1)
    row_flat = row_scale.reshape(-1)
    col_flat = col_scale.reshape(-1)
    scaled_start = (col_flat[:, None] * start_block.astype(jnp.float32)).astype(jnp.bfloat16)
    left_part = tile_pass(
        row_matrix(scaled_start.reshape(CB, TILE, K)), jnp.zeros((RB, TILE, K), jnp.float32)
    )
    left_part = left_part.reshape(RB * TILE, K)
    left_share = RB * TILE // lax.axis_size(DOC)
    left_offset = lax.axis_index(DOC) * left_share
    left_raw, weight_sum = in_one((left_part, weight_part), DOC)
    row_weight = row_flat * weight_sum
    left_block = (
        row_flat[:, None] * left_raw - row_weight[:, None] * start_mean[None, :] / docs_total
    )
    gram_rows = lax.dynamic_slice_in_dim(left_block, left_offset, left_share, 0)
    weight_rows = lax.dynamic_slice_in_dim(row_weight, left_offset, left_share)
    gram_part = jnp.dot(gram_rows.T, gram_rows, precision=PRECISE) / terms_total
    lean_part = jnp.dot(weight_rows, gram_rows, precision=PRECISE)
    left_gram, lean_raw = packed_total(
        (gram_part, lean_part), (("term_0", "term_1", "doc_0"), "doc_1")
    )
    left_inverse = factor_inverse(left_gram)
    lean = jnp.dot(lean_raw, left_inverse, precision=PRECISE)
    left_basis = jnp.dot(left_block, left_inverse, precision=PRECISE).astype(jnp.bfloat16)
    scaled_left = (row_flat[:, None] * left_basis.astype(jnp.float32)).astype(jnp.bfloat16)
    right_part = tile_pass(
        col_matrix(scaled_left.reshape(RB, TILE, K)), jnp.zeros((CB, TILE, K), jnp.float32)
    )
    right_part = right_part.reshape(CB * TILE, K)
    right_share = CB * TILE // lax.axis_size(TERM)
    right_offset = lax.axis_index(TERM) * right_share
    right_raw = total_of(right_part, ("term_0", "term_1"))
    right_block = col_flat[:, None] * right_raw - lean[None, :] / docs_total
    right_rows = lax.dynamic_slice_in_dim(right_block, right_offset, right_share, 0)
    right_gram = total_of(
        jnp.dot(right_rows.T, right_rows, precision=PRECISE) / docs_total,
        (("term_0", "term_1", "doc_0"), "doc_1"),
    )
    right_inverse = factor_inverse(right_gram)
    right_basis = jnp.dot(right_block, right_inverse, precision=PRECISE).astype(jnp.bfloat16)
    return (row_flat, col_flat, left_basis, right_basis)


def solution(mesh):
    torus = Mesh(mesh.devices.reshape(8, 2, 4, 4), ("term_0", "term_1", "doc_0", "doc_1"))
    placed = (P(TERM, DOC, None), P(TERM, DOC), P(TERM, DOC), P(TERM, DOC), P(DOC, None))
    return jax.shard_map(
        per_device,
        mesh=torus,
        in_specs=placed,
        out_specs=(P(TERM), P(DOC), P(TERM, None), P(DOC, None)),
        check_vma=False,
    )
```

profile of v0, /device:TPU:2, one launch (start us, length us, event | category | flops | bytes accessed | tf_op | source)
XLA Modules:
  0.0 613.4 jit_solution(16486611712658080536)
XLA Ops:
  0.6 16.4 %while.95 = (s32[]{:T(128)}, f32[16,128]{1,0:T(8,128)S(1)}, s32[48]{0:T(128)}, bf16[48,128,128]{2,1,0:T(8,128)(2,1)}, s32[48]{0:T(128)}, /*index=5*/s32[]{:T(128...) while((s32[]{:T(128)}, f32[16,128]{1,0:T(8,128)S(1)}, s32[48]{0:T(128)}, ...), condition=%wide.region_2.4_spmd, body=%wide.region_0.3_spmd.sunk | while | flops 3153094 | bytes 603283 | solution.py:131
  17.0 11.0 %psum.42 = f32[16,128]{1,0:T(8,128)S(1)} all-reduce(f32[16,128]{1,0:T(8,128)S(1)} %get-tuple-element.861), channel_id=1, replica_groups=mesh['term_0'=8,'term_1'=2,'doc_0'=4,'doc_1'=4] {'doc_0'}, use_global_device_ids=true, to_apply=%region_3.0 | all-reduce | flops 2048 | bytes 16384 | tf_op jit(solution)/shard_map/psum | solution.py:20
  36.9 15.1 %while.96 = (s32[]{:T(128)}, f32[16,128]{1,0:T(8,128)S(1)}, s32[48]{0:T(128)}, bf16[48,128,128]{2,1,0:T(8,128)(2,1)}, s32[48]{0:T(128)}, /*index=5*/f32[16,128]{...) while((s32[]{:T(128)}, f32[16,128]{1,0:T(8,128)S(1)}, s32[48]{0:T(128)}, ...), condition=%wide.region_7.9_spmd, body=%wide.region_5.0_spmd.sunk | while | flops 3153094 | bytes 595087 | solution.py:131
  70.0 16.3 %while.97 = (s32[]{:T(128)}, f32[16,128]{1,0:T(8,128)S(1)}, s32[48]{0:T(128)}, bf16[48,128,128]{2,1,0:T(8,128)(2,1)}, s32[48]{0:T(128)}, /*index=5*/f32[16,128]{...) while((s32[]{:T(128)}, f32[16,128]{1,0:T(8,128)S(1)}, s32[48]{0:T(128)}, ...), condition=%wide.region_11.13_spmd, body=%wide.region_9.12_spmd.sunk | while | flops 3153094 | bytes 595087 | solution.py:131
  94.4 10.3 %all-reduce.1 = (f32[16,128]{1,0:T(8,128)S(1)}, f32[256]{0:T(256)S(1)}) all-reduce(f32[16,128]{1,0:T(8,128)S(1)} %get-tuple-element.1040, f32[256]{0:T(256)S(1)} %get-tuple-element.1041), channel_id=1, replica_groups=mesh['term_0'=8,'term_1'=2,'doc_0'=4,'doc_1'=4] {'doc_1'}, use_global_device_ids=true, to_apply=%region_13.15 | all-reduce | flops 2304 | bytes 18432 | tf_op jit(solution)/shard_map/psum | solution.py:20
  104.7 15.1 %while.98 = (s32[]{:T(128)}, f32[16,128]{1,0:T(8,128)S(1)}, s32[48]{0:T(128)}, bf16[48,128,128]{2,1,0:T(8,128)(2,1)}, s32[48]{0:T(128)}, /*index=5*/f32[16,128]{...) while((s32[]{:T(128)}, f32[16,128]{1,0:T(8,128)S(1)}, s32[48]{0:T(128)}, ...), condition=%wide.region_16.18_spmd, body=%wide.region_14.17_spmd.sunk | while | flops 3153094 | bytes 595087 | solution.py:131
  135.6 29.2 %while.99 = (s32[]{:T(128)}, f32[16,128,256]{2,1,0:T(8,128)}, s32[48]{0:T(128)S(1)}, bf16[48,128,128]{2,1,0:T(8,128)(2,1)S(1)}, s32[48]{0:T(128)S(1)}, /*index=5...) while((s32[]{:T(128)}, f32[16,128,256]{2,1,0:T(8,128)}, ...), condition=%wide.region_20.0_spmd, body=%wide.region_18.0_spmd.sunk | while | flops 135791808 | bytes 12064447 | solution.py:131
  179.9 33.0 %all_to_all.99 = f32[16,1,32896]{2,1,0:T(1,128)} all-to-all(f32[16,1,32896]{2,1,0:T(1,128)S(1)} %bitcast.179), channel_id=1, replica_groups=mesh['term_0'=8,'term_1'=2,'doc_0'=4,'doc_1'=4] {'doc_0','doc_1'}, dimensions={0} | all-to-all | bytes 4210688 | tf_op jit(solution)/shard_map/all_to_all | solution.py:40
  224.3 27.4 %all-to-all-done.3 = f32[16,1,32896]{2,1,0:T(1,128)} async-done(((f32[16,1,32896]{2,1,0:T(1,128)}), f32[16,1,32896]{2,1,0:T(1,128)}, u32[]{:S(2)}, u32[]{:S(2)}) %all-to-all-start.3) | async-done | bytes 2105376 | tf_op jit(solution)/shard_map/all_to_all | solution.py:26
  268.1 13.4 %all_to_all.100 = f32[4,64,257]{2,1,0:T(8,128)S(1)} all-to-all(f32[4,64,257]{2,1,0:T(8,128)S(1)} %copy.47), channel_id=1, replica_groups=mesh['term_0'=8,'term_1'=2,'doc_0'=4,'doc_1'=4] {'doc_1'}, dimensions={0} | all-to-all | bytes 526336 | tf_op jit(solution)/shard_map/all_to_all | solution.py:40
  281.6 14.7 %all_to_all.101 = f32[64,1,257]{2,1,0:T(1,128)S(1)} all-to-all(f32[64,1,257]{2,1,0:T(1,128)S(1)} %all_to_all.66), channel_id=1, replica_groups=mesh['term_0'=8,'term_1'=2,'doc_0'=4,'doc_1'=4] {'term_0','term_1','doc_0'}, dimensions={0} | all-to-all | bytes 131584 | tf_op jit(solution)/shard_map/all_to_all | solution.py:79
  301.6 10.8 %all-to-all-done.6 = f32[64,1,257]{2,1,0:T(1,128)S(1)} async-done(((f32[64,1,257]{2,1,0:T(1,128)}), f32[64,1,257]{2,1,0:T(1,128)S(1)}, u32[]{:S(2)}, u32[]{:S(2)}) %all-to-all-start.6) | async-done | bytes 65824 | tf_op jit(solution)/shard_map/all_to_all | solution.py:26
  325.4 11.7 %cholesky.130 = f32[128,128]{1,0:T(8,128)S(1)} custom-call(f32[128,128]{1,0:T(8,128)S(1)} %cholesky.194), custom_call_target="Cholesky" | custom-call | tf_op jit(solution)/shard_map/jit(cholesky)/cholesky | solution.py:111
  337.2 9.8 %custom-call.13 = f32[1,128,128]{1,2,0:T(8,128)S(1)} custom-call(f32[1,128,128]{2,1,0:T(8,128)S(1)} %get-tuple-element.1076), custom_call_target="InvertDiagBlocksLowerTriangular" | custom-call | tf_op jit(solution)/shard_map/jit(cholesky)/cholesky | solution.py:111
  347.5 11.7 %cholesky.147 = f32[128,128]{1,0:T(8,128)S(1)} custom-call(f32[128,128]{1,0:T(8,128)S(1)} %convolution_subtract_fusion.3), custom_call_target="Cholesky" | custom-call | tf_op jit(solution)/shard_map/jit(cholesky)/cholesky | solution.py:111
  365.6 19.8 %custom-call.14 = f32[2,128,128]{1,2,0:T(8,128)S(1)} custom-call(f32[2,128,128]{2,1,0:T(8,128)S(1)} %get-tuple-element.882), custom_call_target="InvertDiagBlocksLowerTriangular" | custom-call | tf_op jit(solution)/shard_map/jit(_solve_triangular)/triangular_solve | solution.py:113
  392.8 29.1 %while.101 = (s32[]{:T(128)}, f32[16,128,256]{2,1,0:T(8,128)}, s32[48]{0:T(128)S(1)}, bf16[48,128,128]{2,1,0:T(8,128)(2,1)S(1)}, s32[48]{0:T(128)S(1)}, /*index=...) while((s32[]{:T(128)}, f32[16,128,256]{2,1,0:T(8,128)}, ...), condition=%wide.region_36.41_spmd, body=%wide.region_34.0_spmd.sunk | while | flops 135791808 | bytes 12064447 | solution.py:131
  429.2 32.0 %all_to_all.102 = f32[8,128,256]{2,1,0:T(8,128)S(1)} all-to-all(f32[8,128,256]{2,1,0:T(8,128)S(1)} %reduce_sum.98), channel_id=1, replica_groups=mesh['term_0'=8,'term_1'=2,'doc_0'=4,'doc_1'=4] {'term_0'}, dimensions={0} | all-to-all | bytes 2097152 | tf_op jit(solution)/shard_map/all_to_all | solution.py:79
  466.7 27.1 %all-to-all-done.10 = f32[8,128,256]{2,1,0:T(8,128)S(1)} async-done(((f32[8,128,256]{2,1,0:T(8,128)}), f32[8,128,256]{2,1,0:T(8,128)S(1)}, u32[]{:S(2)}, u32[]{:S(2)}) %all-to-all-start.10) | async-done | bytes 1048608 | tf_op jit(solution)/shard_map/all_to_all | solution.py:26
  510.2 14.9 %all_to_all.104 = f32[64,1,256]{2,1,0:T(1,128)S(1)} all-to-all(f32[64,1,256]{2,1,0:T(1,128)S(1)} %reduce_sum.101), channel_id=1, replica_groups=mesh['term_0'=8,'term_1'=2,'doc_0'=4,'doc_1'=4] {'term_0','term_1','doc_0'}, dimensions={0} | all-to-all | bytes 131072 | tf_op jit(solution)/shard_map/all_to_all | solution.py:79
  525.3 13.9 %all_to_all.98 = f32[64,1,256]{2,1,0:T(1,128)S(1)} all-to-all(f32[64,1,256]{2,1,0:T(1,128)S(1)} %broadcast_in_dim.126), channel_id=1, replica_groups=mesh['term_0'=8,'term_1'=2,'doc_0'=4,'doc_1'=4] {'term_0','term_1','doc_0'}, dimensions={0} | all-to-all | bytes 131072 | tf_op jit(solution)/shard_map/all_to_all | solution.py:26
  549.0 11.7 %cholesky.164 = f32[128,128]{1,0:T(8,128)S(1)} custom-call(f32[128,128]{1,0:T(8,128)S(1)} %cholesky.197), custom_call_target="Cholesky" | custom-call | tf_op jit(solution)/shard_map/jit(cholesky)/cholesky | solution.py:111
  571.1 11.7 %cholesky.181 = f32[128,128]{1,0:T(8,128)S(1)} custom-call(f32[128,128]{1,0:T(8,128)S(1)} %convolution_subtract_fusion.2), custom_call_target="Cholesky" | custom-call | tf_op jit(solution)/shard_map/jit(cholesky)/cholesky | solution.py:111
  589.3 19.9 %custom-call.16 = f32[2,128,128]{1,2,0:T(8,128)S(1)} custom-call(f32[2,128,128]{2,1,0:T(8,128)S(1)} %get-tuple-element.883), custom_call_target="InvertDiagBlocksLowerTriangular" | custom-call | tf_op jit(solution)/shard_map/jit(_solve_triangular)/triangular_solve | solution.py:113
  (301 shorter events, 320.5 us)
Async XLA Ops:
  17.0 44.2 %copy-start.2 = (bf16[2048,256]{1,0:T(8,128)(2,1)S(1)}, bf16[2048,256]{1,0:T(8,128)(2,1)}, u32[]{:S(2)}) copy-start(bf16[2048,256]{1,0:T(8,128)(2,1)} %param.30) | copy-start | bytes 3145732
  52.7 17.3 %all-to-all-start = ((f32[16,16,128]{2,1,0:T(8,128)}), f32[16,16,128]{2,1,0:T(8,128)S(1)}, u32[]{:S(2)}, u32[]{:S(2)}) async-start(f32[16,16,128]{2,1,0:T(8,128)} %broadcast_in_dim.119), calls=%async_computation | async-start | bytes 262144 | tf_op jit(solution)/shard_map/all_to_all | solution.py:26
  120.5 12.2 %all-to-all-start.1 = ((f32[16,16,128]{2,1,0:T(8,128)}), f32[16,16,128]{2,1,0:T(8,128)S(1)}, u32[]{:S(2)}, u32[]{:S(2)}) async-start(f32[16,16,128]{2,1,0:T(8,128)} %broadcast_in_dim.120), calls=%async_computation.1 | async-start | bytes 262144 | tf_op jit(solution)/shard_map/all_to_all | solution.py:26
  132.8 366.9 %copy-start.11 = (f32[2048]{0:T(1024)}, f32[2048]{0:T(1024)S(1)}, u32[]{:S(2)}) copy-start(f32[2048]{0:T(1024)S(1)} %get-tuple-element.1077) | copy-start | bytes 24580
  132.8 2.9 copy-start
  132.8 2.9 copy-start.9
  132.8 2.8 copy-start.10
  218.2 33.5 %all-to-all-start.3 = ((f32[16,1,32896]{2,1,0:T(1,128)}), f32[16,1,32896]{2,1,0:T(1,128)}, u32[]{:S(2)}, u32[]{:S(2)}) async-start(f32[16,1,32896]{2,1,0:T(1,128)} %broadcast_in_dim.121), calls=%async_computation.3 | async-start | bytes 4210688 | tf_op jit(solution)/shard_map/all_to_all | solution.py:26
  263.8 122.5 %copy-start.12 = (f32[2048]{0:T(1024)}, f32[2048]{0:T(1024)S(1)}, u32[]{:S(2)}) copy-start(f32[2048]{0:T(1024)S(1)} %get-tuple-element.1057) | copy-start | bytes 24580
  265.8 1.4 copy-start.1
  297.0 15.4 %all-to-all-start.6 = ((f32[64,1,257]{2,1,0:T(1,128)}), f32[64,1,257]{2,1,0:T(1,128)S(1)}, u32[]{:S(2)}, u32[]{:S(2)}) async-start(f32[64,1,257]{2,1,0:T(1,128)} %broadcast_in_dim.122), calls=%async_computation.6 | async-start | bytes 196608 | tf_op jit(solution)/shard_map/all_to_all | solution.py:26
  313.2 11.2 %all-to-all-start.7 = ((f32[4,64,257]{2,1,0:T(8,128)}), f32[4,64,257]{2,1,0:T(8,128)S(1)}, u32[]{:S(2)}, u32[]{:S(2)}) async-start(f32[4,64,257]{2,1,0:T(8,128)} %broadcast_in_dim.123), calls=%async_computation.7 | async-start | bytes 786432 | tf_op jit(solution)/shard_map/all_to_all | solution.py:26
  318.5 67.3 %copy-start.3 = (f32[256,256]{1,0:T(8,128)}, f32[256,256]{1,0:T(8,128)S(1)}, u32[]{:S(2)}) copy-start(f32[256,256]{1,0:T(8,128)S(1)} %fusion.53) | copy-start | bytes 786436
  365.1 0.6 copy-start.13
  385.8 5.4 copy-start.5
  386.4 4.8 copy-start.7
  461.3 5.1 copy-start.6
  461.3 5.1 copy-start.8
  462.4 31.4 %all-to-all-start.10 = ((f32[8,128,256]{2,1,0:T(8,128)}), f32[8,128,256]{2,1,0:T(8,128)S(1)}, u32[]{:S(2)}, u32[]{:S(2)}) async-start(f32[8,128,256]{2,1,0:T(8,128)} %broadcast_in_dim.124), calls=%async_computation.10 | async-start | bytes 2097152 | tf_op jit(solution)/shard_map/all_to_all | solution.py:26
  548.5 36.9 %copy-start.14 = (s32[2,2]{1,0:T(2,128)S(1)}, s32[2,2]{1,0:T(2,128)}, u32[]{:S(2)}) copy-start(s32[2,2]{1,0:T(2,128)} %copy-done.13) | copy-start | bytes 52
  548.8 60.4 %copy-start.4 = (f32[256,256]{1,0:T(8,128)S(1)}, f32[256,256]{1,0:T(8,128)}, u32[]{:S(2)}) copy-start(f32[256,256]{1,0:T(8,128)} %copy-done.3) | copy-start | bytes 786436
where the time goes:
time: 624 us; the launch traced here: 613 us
  other arithmetic  202 us (32%)
  blocking collectives  190 us (30%)
  waiting for transfers between devices  88.3 us (14%)
  local copies, waits for them, and re-layouts  50.5 us (8%)
  matrix products  46.4 us (7%)
  starting transfers between devices  31.6 us (5%)
    all_to_all x6, waiting for transfers between devices, sent_to_all(): return lax.all_to_all(copies, axis, split_axis=0, concat_axis=0, tiled=True)  88.3 us
    another operation x13, other arithmetic, factor_inverse(): lower = jnp.linalg.cholesky(gram)  68.5 us
    all_to_all x3, blocking collectives, summed_rows(): lax.all_to_all(nearer, far, split_axis=0, concat_axis=0, tiled=True)  61.6 us
    all_to_all x4, blocking collectives, summed_on_arrival(): lax.all_to_all(pieces, axis, split_axis=0, concat_axis=0, tiled=True)  61.4 us
    another operation x5, other arithmetic, factor_inverse(): return jax.scipy.linalg.solve_triangular(lower, identity, lower=True).T  39.8 us
    psum x4, blocking collectives, by_axis(): shard = lax.psum(shard, axis)  38 us
    all_to_all x6, starting transfers between devices, sent_to_all(): return lax.all_to_all(copies, axis, split_axis=0, concat_axis=0, tiled=True)  31.6 us
    all_to_all x3, blocking collectives, sent_to_all(): return lax.all_to_all(copies, axis, split_axis=0, concat_axis=0, tiled=True)  28.6 us
  transfers between devices with their start and end apart: 6, of which 6 were waited for; matrix products, arithmetic and copies ran while one was open for 0% of the time, Pallas kernels for 0%

commit v1 on v0

--- a/solution.py
+++ b/solution.py
@@ -17,7 +17,7 @@
 
 def by_axis(shard, axes):
     for axis in axes:
-        shard = lax.psum(shard, axis)
+        shard = jnp.sum(lax.all_gather(shard, axis), axis=0)
     return shard
 
 

time: 624 us -> 651 us (1.043)
  blocking collectives: 190 us -> 236 us
  waiting for transfers between devices: 88.3 us -> 61.2 us
    all_gather x0 -> x6, blocking collectives: none -> 84.5 us  [by_axis(): shard = jnp.sum(lax.all_gather(shard, axis), axis=0)]
    psum x4 -> x0, blocking collectives: 38 us -> none  [by_axis(): shard = lax.psum(shard, axis)]
    all_to_all x6, waiting for transfers between devices: 88.3 us -> 61.2 us  [sent_to_all(): return lax.all_to_all(copies, axis, split_axis=0, concat_axis=0, tiled=True)]
  transfers between devices with their start and end apart: 6 -> 6, of which waited for: 6 -> 5; matrix products, arithmetic and copies ran while one was open for 0% -> 0% of each run, Pallas kernels for 0% -> 0%
where the time goes in v1:
time: 651 us; the launch traced here: 641 us
  blocking collectives  236 us (36%)
  other arithmetic  205 us (31%)
  waiting for transfers between devices  61.2 us (9%)
  local copies, waits for them, and re-layouts  51.8 us (8%)
  matrix products  50.1 us (8%)
  starting transfers between devices  31.2 us (5%)
    all_gather x6, blocking collectives, by_axis(): shard = jnp.sum(lax.all_gather(shard, axis), axis=0)  84.5 us
    another operation x13, other arithmetic, factor_inverse(): lower = jnp.linalg.cholesky(gram)  68.5 us
    all_to_all x4, blocking collectives, summed_on_arrival(): lax.all_to_all(pieces, axis, split_axis=0, concat_axis=0, tiled=True)  61.7 us
    all_to_all x3, blocking collectives, summed_rows(): lax.all_to_all(nearer, far, split_axis=0, concat_axis=0, tiled=True)  61.4 us
    all_to_all x6, waiting for transfers between devices, sent_to_all(): return lax.all_to_all(copies, axis, split_axis=0, concat_axis=0, tiled=True)  61.2 us
    another operation x5, other arithmetic, factor_inverse(): return jax.scipy.linalg.solve_triangular(lower, identity, lower=True).T  39.8 us
    all_to_all x6, starting transfers between devices, sent_to_all(): return lax.all_to_all(copies, axis, split_axis=0, concat_axis=0, tiled=True)  31.2 us
    all_to_all x3, blocking collectives, sent_to_all(): return lax.all_to_all(copies, axis, split_axis=0, concat_axis=0, tiled=True)  28.6 us
  transfers between devices with their start and end apart: 6, of which 5 were waited for; matrix products, arithmetic and copies ran while one was open for 0% of the time, Pallas kernels for 0%

profile of v1, /device:TPU:2, one launch (start us, length us, event | category | flops | bytes accessed | tf_op | source)
XLA Modules:
  0.0 640.8 jit_solution(11249959921658904668)
XLA Ops:
  0.6 16.4 %while.95 = (s32[]{:T(128)}, f32[16,128]{1,0:T(8,128)S(1)}, s32[48]{0:T(128)}, bf16[48,128,128]{2,1,0:T(8,128)(2,1)}, s32[48]{0:T(128)}, /*index=5*/s32[]{:T(128...) while((s32[]{:T(128)}, f32[16,128]{1,0:T(8,128)S(1)}, s32[48]{0:T(128)}, ...), condition=%wide.region_2.4_spmd, body=%wide.region_0.3_spmd.sunk | while | flops 3153094 | bytes 603283 | solution.py:131
  17.0 12.4 %all-gather = f32[64,128]{1,0:T(8,128)S(1)} all-gather(f32[16,128]{1,0:T(8,128)S(1)} %get-tuple-element.861), channel_id=2, replica_groups=mesh['term_0'=8,'term_1'=2,'doc_0'=4,'doc_1'=4] {'doc_0'}, dimensions={0}, use_global_device_ids=true | all-gather | bytes 40960 | tf_op jit(solution)/shard_map/all_gather | solution.py:20
  29.5 12.0 %all-gather.1 = f32[64,128]{1,0:T(8,128)S(1)} all-gather(f32[16,128]{1,0:T(8,128)S(1)} %reduce_sum.146), channel_id=3, replica_groups=mesh['term_0'=8,'term_1'=2,'doc_0'=4,'doc_1'=4] {'doc_1'}, dimensions={0}, use_global_device_ids=true | all-gather | bytes 40960 | tf_op jit(solution)/shard_map/all_gather | solution.py:20
  41.5 15.1 %while.96 = (s32[]{:T(128)}, f32[16,128]{1,0:T(8,128)S(1)}, s32[48]{0:T(128)}, bf16[48,128,128]{2,1,0:T(8,128)(2,1)}, s32[48]{0:T(128)}, /*index=5*/f32[16,128]{...) while((s32[]{:T(128)}, f32[16,128]{1,0:T(8,128)S(1)}, s32[48]{0:T(128)}, ...), condition=%wide.region_7.9_spmd, body=%wide.region_5.0_spmd.sunk | while | flops 3153094 | bytes 595087 | solution.py:131
  74.6 16.3 %while.97 = (s32[]{:T(128)}, f32[16,128]{1,0:T(8,128)S(1)}, s32[48]{0:T(128)}, bf16[48,128,128]{2,1,0:T(8,128)(2,1)}, s32[48]{0:T(128)}, /*index=5*/f32[16,128]{...) while((s32[]{:T(128)}, f32[16,128]{1,0:T(8,128)S(1)}, s32[48]{0:T(128)}, ...), condition=%wide.region_11.13_spmd, body=%wide.region_9.12_spmd.sunk | while | flops 3153094 | bytes 595087 | solution.py:131
  91.0 11.9 %all-gather.2 = f32[64,128]{1,0:T(8,128)S(1)} all-gather(f32[16,128]{1,0:T(8,128)S(1)} %get-tuple-element.863), channel_id=4, replica_groups=mesh['term_0'=8,'term_1'=2,'doc_0'=4,'doc_1'=4] {'doc_0'}, dimensions={0}, use_global_device_ids=true | all-gather | bytes 40960 | tf_op jit(solution)/shard_map/all_gather | solution.py:20
  102.9 11.9 %all-gather.3 = f32[64,128]{1,0:T(8,128)S(1)} all-gather(f32[16,128]{1,0:T(8,128)S(1)} %reduce_sum.149), channel_id=5, replica_groups=mesh['term_0'=8,'term_1'=2,'doc_0'=4,'doc_1'=4] {'doc_1'}, dimensions={0}, use_global_device_ids=true | all-gather | bytes 40960 | tf_op jit(solution)/shard_map/all_gather | solution.py:20
  114.8 15.2 %while.98 = (s32[]{:T(128)}, f32[16,128]{1,0:T(8,128)S(1)}, s32[48]{0:T(128)}, bf16[48,128,128]{2,1,0:T(8,128)(2,1)}, s32[48]{0:T(128)}, /*index=5*/f32[16,128]{...) while((s32[]{:T(128)}, f32[16,128]{1,0:T(8,128)S(1)}, s32[48]{0:T(128)}, ...), condition=%wide.region_16.18_spmd, body=%wide.region_14.17_spmd.sunk | while | flops 3153094 | bytes 595087 | solution.py:131
  146.1 29.2 %while.99 = (s32[]{:T(128)}, f32[16,128,256]{2,1,0:T(8,128)}, s32[48]{0:T(128)S(1)}, bf16[48,128,128]{2,1,0:T(8,128)(2,1)S(1)}, s32[48]{0:T(128)S(1)}, /*index=5...) while((s32[]{:T(128)}, f32[16,128,256]{2,1,0:T(8,128)}, ...), condition=%wide.region_20.0_spmd, body=%wide.region_18.0_spmd.sunk | while | flops 135791808 | bytes 12064447 | solution.py:131
  190.4 34.8 %all_to_all.99 = f32[16,1,32896]{2,1,0:T(1,128)} all-to-all(f32[16,1,32896]{2,1,0:T(1,128)S(1)} %bitcast.185), channel_id=1, replica_groups=mesh['term_0'=8,'term_1'=2,'doc_0'=4,'doc_1'=4] {'doc_0','doc_1'}, dimensions={0} | all-to-all | bytes 4210688 | tf_op jit(solution)/shard_map/all_to_all | solution.py:40
  236.1 20.8 %all-gather.6 = f32[4,1,256]{2,1,0:T(1,128)S(1)} all-gather(f32[1,1,256]{2,1,0:T(1,128)S(1)} %bitcast.212), channel_id=6, replica_groups=mesh['term_0'=8,'term_1'=2,'doc_0'=4,'doc_1'=4] {'doc_0'}, dimensions={0}, use_global_device_ids=true | all-gather | bytes 5120 | tf_op jit(solution)/shard_map/all_gather | solution.py:20
  257.0 15.5 %all-gather.7 = f32[4,1,256]{2,1,0:T(1,128)S(1)} all-gather(f32[1,1,256]{2,1,0:T(1,128)S(1)} %bitcast.215), channel_id=7, replica_groups=mesh['term_0'=8,'term_1'=2,'doc_0'=4,'doc_1'=4] {'doc_1'}, dimensions={0}, use_global_device_ids=true | all-gather | bytes 5120 | tf_op jit(solution)/shard_map/all_gather | solution.py:20
  300.1 14.6 %all_to_all.101 = f32[64,1,257]{2,1,0:T(1,128)S(1)} all-to-all(f32[64,1,257]{2,1,0:T(1,128)S(1)} %all_to_all.66), channel_id=1, replica_groups=mesh['term_0'=8,'term_1'=2,'doc_0'=4,'doc_1'=4] {'term_0','term_1','doc_0'}, dimensions={0} | all-to-all | bytes 131584 | tf_op jit(solution)/shard_map/all_to_all | solution.py:79
  343.8 11.7 %cholesky.130 = f32[128,128]{1,0:T(8,128)S(1)} custom-call(f32[128,128]{1,0:T(8,128)S(1)} %cholesky.194), custom_call_target="Cholesky" | custom-call | tf_op jit(solution)/shard_map/jit(cholesky)/cholesky | solution.py:111
  365.9 11.7 %cholesky.147 = f32[128,128]{1,0:T(8,128)S(1)} custom-call(f32[128,128]{1,0:T(8,128)S(1)} %convolution_subtract_fusion.3), custom_call_target="Cholesky" | custom-call | tf_op jit(solution)/shard_map/jit(cholesky)/cholesky | solution.py:111
  383.6 19.8 %custom-call.14 = f32[2,128,128]{1,2,0:T(8,128)S(1)} custom-call(f32[2,128,128]{2,1,0:T(8,128)S(1)} %get-tuple-element.882), custom_call_target="InvertDiagBlocksLowerTriangular" | custom-call | tf_op jit(solution)/shard_map/jit(_solve_triangular)/triangular_solve | solution.py:113
  410.7 32.7 %while.101 = (s32[]{:T(128)}, f32[16,128,256]{2,1,0:T(8,128)}, s32[48]{0:T(128)S(1)}, bf16[48,128,128]{2,1,0:T(8,128)(2,1)S(1)}, s32[48]{0:T(128)S(1)}, /*index=...) while((s32[]{:T(128)}, f32[16,128,256]{2,1,0:T(8,128)}, ...), condition=%wide.region_36.41_spmd, body=%wide.region_34.0_spmd.sunk | while | flops 135791808 | bytes 12063999 | solution.py:131
  453.3 32.0 %all_to_all.102 = f32[8,128,256]{2,1,0:T(8,128)S(1)} all-to-all(f32[8,128,256]{2,1,0:T(8,128)S(1)} %reduce_sum.158), channel_id=1, replica_groups=mesh['term_0'=8,'term_1'=2,'doc_0'=4,'doc_1'=4] {'term_0'}, dimensions={0} | all-to-all | bytes 2097152 | tf_op jit(solution)/shard_map/all_to_all | solution.py:79
  490.7 27.1 %all-to-all-done.10 = f32[8,128,256]{2,1,0:T(8,128)S(1)} async-done(((f32[8,128,256]{2,1,0:T(8,128)}), f32[8,128,256]{2,1,0:T(8,128)S(1)}, u32[]{:S(2)}, u32[]{:S(2)}) %all-to-all-start.10) | async-done | bytes 1048608 | tf_op jit(solution)/shard_map/all_to_all | solution.py:26
  536.0 14.9 %all_to_all.104 = f32[64,1,256]{2,1,0:T(1,128)S(1)} all-to-all(f32[64,1,256]{2,1,0:T(1,128)S(1)} %reduce_sum.161), channel_id=1, replica_groups=mesh['term_0'=8,'term_1'=2,'doc_0'=4,'doc_1'=4] {'term_0','term_1','doc_0'}, dimensions={0} | all-to-all | bytes 131072 | tf_op jit(solution)/shard_map/all_to_all | solution.py:79
  551.0 13.9 %all_to_all.98 = f32[64,1,256]{2,1,0:T(1,128)S(1)} all-to-all(f32[64,1,256]{2,1,0:T(1,128)S(1)} %broadcast_in_dim.126), channel_id=1, replica_groups=mesh['term_0'=8,'term_1'=2,'doc_0'=4,'doc_1'=4] {'term_0','term_1','doc_0'}, dimensions={0} | all-to-all | bytes 131072 | tf_op jit(solution)/shard_map/all_to_all | solution.py:26
  574.7 11.7 %cholesky.164 = f32[128,128]{1,0:T(8,128)S(1)} custom-call(f32[128,128]{1,0:T(8,128)S(1)} %cholesky.197), custom_call_target="Cholesky" | custom-call | tf_op jit(solution)/shard_map/jit(cholesky)/cholesky | solution.py:111
  596.8 11.7 %cholesky.181 = f32[128,128]{1,0:T(8,128)S(1)} custom-call(f32[128,128]{1,0:T(8,128)S(1)} %convolution_subtract_fusion.2), custom_call_target="Cholesky" | custom-call | tf_op jit(solution)/shard_map/jit(cholesky)/cholesky | solution.py:111
  615.1 19.9 %custom-call.16 = f32[2,128,128]{1,2,0:T(8,128)S(1)} custom-call(f32[2,128,128]{2,1,0:T(8,128)S(1)} %get-tuple-element.883), custom_call_target="InvertDiagBlocksLowerTriangular" | custom-call | tf_op jit(solution)/shard_map/jit(_solve_triangular)/triangular_solve | solution.py:113
  (300 shorter events, 344.6 us)
Async XLA Ops:
  57.3 17.3 %all-to-all-start = ((f32[16,16,128]{2,1,0:T(8,128)}), f32[16,16,128]{2,1,0:T(8,128)S(1)}, u32[]{:S(2)}, u32[]{:S(2)}) async-start(f32[16,16,128]{2,1,0:T(8,128)} %broadcast_in_dim.119), calls=%async_computation | async-start | bytes 262144 | tf_op jit(solution)/shard_map/all_to_all | solution.py:26
  114.8 28.2 %copy-start.3 = (bf16[2048,256]{1,0:T(8,128)(2,1)S(1)}, bf16[2048,256]{1,0:T(8,128)(2,1)}, u32[]{:S(2)}) copy-start(bf16[2048,256]{1,0:T(8,128)(2,1)} %param.30) | copy-start | bytes 3145732
  130.7 12.2 %all-to-all-start.1 = ((f32[16,16,128]{2,1,0:T(8,128)}), f32[16,16,128]{2,1,0:T(8,128)S(1)}, u32[]{:S(2)}, u32[]{:S(2)}) async-start(f32[16,16,128]{2,1,0:T(8,128)} %broadcast_in_dim.120), calls=%async_computation.1 | async-start | bytes 262144 | tf_op jit(solution)/shard_map/all_to_all | solution.py:26
  143.0 3.1 copy-start.6
  143.0 3.1 copy-start
  143.0 3.1 copy-start.4
  143.0 3.0 copy-start.5
  230.4 42.1 %all-to-all-start.3 = ((f32[16,1,32896]{2,1,0:T(1,128)}), f32[16,1,32896]{2,1,0:T(1,128)}, u32[]{:S(2)}, u32[]{:S(2)}) async-start(f32[16,1,32896]{2,1,0:T(1,128)} %broadcast_in_dim.121), calls=%async_computation.3 | async-start | bytes 4210688 | tf_op jit(solution)/shard_map/all_to_all | solution.py:26
  284.6 119.7 %copy-start.8 = (f32[2048]{0:T(1024)}, f32[2048]{0:T(1024)S(1)}, u32[]{:S(2)}) copy-start(f32[2048]{0:T(1024)S(1)} %get-tuple-element.1053) | copy-start | bytes 24580
  286.6 1.4 copy-start.1
  315.4 15.4 %all-to-all-start.6 = ((f32[64,1,257]{2,1,0:T(1,128)}), f32[64,1,257]{2,1,0:T(1,128)S(1)}, u32[]{:S(2)}, u32[]{:S(2)}) async-start(f32[64,1,257]{2,1,0:T(1,128)} %broadcast_in_dim.122), calls=%async_computation.6 | async-start | bytes 196608 | tf_op jit(solution)/shard_map/all_to_all | solution.py:26
  331.6 11.2 %all-to-all-start.7 = ((f32[4,64,257]{2,1,0:T(8,128)}), f32[4,64,257]{2,1,0:T(8,128)S(1)}, u32[]{:S(2)}, u32[]{:S(2)}) async-start(f32[4,64,257]{2,1,0:T(8,128)} %broadcast_in_dim.123), calls=%async_computation.7 | async-start | bytes 786432 | tf_op jit(solution)/shard_map/all_to_all | solution.py:26
  383.6 25.5 %copy-start.9 = (s32[2,2]{1,0:T(2,128)}, s32[2,2]{1,0:T(2,128)S(1)}, u32[]{:S(2)}) copy-start(s32[2,2]{1,0:T(2,128)S(1)} %get-tuple-element.1768) | copy-start | bytes 52
  486.4 31.4 %all-to-all-start.10 = ((f32[8,128,256]{2,1,0:T(8,128)}), f32[8,128,256]{2,1,0:T(8,128)S(1)}, u32[]{:S(2)}, u32[]{:S(2)}) async-start(f32[8,128,256]{2,1,0:T(8,128)} %broadcast_in_dim.124), calls=%async_computation.10 | async-start | bytes 2097152 | tf_op jit(solution)/shard_map/all_to_all | solution.py:26
  523.4 0.7 copy-start.7
  524.5 1.4 copy-start.2
  574.3 36.9 %copy-start.10 = (s32[2,2]{1,0:T(2,128)S(1)}, s32[2,2]{1,0:T(2,128)}, u32[]{:S(2)}) copy-start(s32[2,2]{1,0:T(2,128)} %copy-done.9) | copy-start | bytes 52
